TPU v7x, 32 devices: a whole 2x2x4 slice. The times are simulated.
32 devices in a mesh: grp: 2 (over x), ch: 4 (over y, core), sp: 4 (over z).
Axes of the slice: x: 2, y: 2, z: 4, core: 2. Of those that a mesh axis runs over, the one named last changes fastest.
Arguments:
- features: bfloat16 [1024, 64, 128], P(('grp', 'ch'), 'sp'), parts along dimension 0, may hold values from -6 to 6
- saved_mix: bfloat16 [1024, 64, 128], P(('grp', 'ch'), 'sp'), parts along dimension 0, may hold values from -6 to 6
- out_grad: bfloat16 [1024, 64, 128], P(('grp', 'ch'), 'sp'), parts along dimension 0, may hold values from -6 to 6
- kernel: bfloat16 [512, 31, 31], P('ch'), may hold values from -0.1875 to 0.1875
- w_in: bfloat16 [512, 2048], P(None, 'ch'), may hold values from -0.25 to 0.25
- w_out: bfloat16 [2048, 512], P('ch'), may hold values from -0.125 to 0.125
Outputs:
- in_grad: float32 [1024, 64, 128], P(('grp', 'ch'), 'sp'), parts along dimension 0
- kernel_grad: float32 [1024, 31, 31], P(('grp', 'ch')), parts along dimension 0
- w_in_grad: float32 [1024, 2048], P('grp', ('ch', 'sp')), parts along dimension 0
- w_out_grad: float32 [4096, 512], P(('grp', 'ch', 'sp')), parts along dimension 0
There are 2 independent parts, one for each index of `grp`. A program takes and returns all parts, laid end to end along the dimension named above; an argument that names none is the same for every part. Nothing has to cross between parts.
All inputs are finite; a program needn't handle non-finite values.
Results may differ from a plain program's by a relative error of at most 0.0041.
Values may be sent and summed in bfloat16 or wider, within the bound.
A program may use at most 64 MiB of HBM per device.

v0:
```python
import math
import jax
import jax.numpy as jnp
from jax import lax
from jax.sharding import PartitionSpec as P

SQRT_HALF = 0.7071067811865476
INV_ROOT_TAU = 0.3989422804014327


def with_halo(block, sides, width):
    for axis, dim in sides:
        count = lax.axis_size(axis)
        forward = [(i, i + 1) for i in range(count - 1)]
        backward = [(target, source) for source, target in forward]
        low = lax.ppermute(
            lax.slice_in_dim(block, block.shape[dim] - width, None, axis=dim), axis, forward
        )
        high = lax.ppermute(lax.slice_in_dim(block, 0, width, axis=dim), axis, backward)
        block = jnp.concatenate([low, block, high], axis=dim)
    return block


def depthwise(source, taps):
    return lax.conv_general_dilated(
        source[None],
        taps[:, None],
        (1, 1),
        "VALID",
        dimension_numbers=("NCHW", "OIHW", "NCHW"),
        feature_group_count=source.shape[0],
        preferred_element_type=jnp.float32,
    )[0]


def contract_last(left, right):
    return lax.dot_general(
        left, right, (((1,), (1,)), ((), ())), preferred_element_type=jnp.float32
    )


def contract_first(left, right):
    return lax.dot_general(
        left, right, (((0,), (0,)), ((), ())), preferred_element_type=jnp.float32
    )


def pointwise_back(mixed_rows, grad_rows, w_in_block, w_out_block):
    preact = contract_first(w_in_block, mixed_rows)
    normal_cdf = 0.5 * (1.0 + jax.scipy.special.erf(preact * SQRT_HALF))
    normal_pdf = INV_ROOT_TAU * jnp.exp(-0.5 * preact * preact)
    hidden = (preact * normal_cdf).astype(jnp.bfloat16)
    hidden_grad = jnp.dot(w_out_block, grad_rows, preferred_element_type=jnp.float32)
    preact_grad = (hidden_grad * (normal_cdf + preact * normal_pdf)).astype(jnp.bfloat16)
    return (hidden, preact_grad)


def per_device(features, saved_mix, out_grad, kernel, w_in, w_out):
    local_ch, rows, width = features.shape
    local_pos = rows * width
    half = kernel.shape[1] // 2
    factor = 1.0 / math.sqrt(local_pos * lax.axis_size("sp"))
    mixed_rows = saved_mix.reshape(local_ch, local_pos)
    grad_rows = out_grad.reshape(local_ch, local_pos)
    mixed_all, grad_all = (
        lax.all_gather(mixed_rows, "ch", axis=0, tiled=True),
        lax.all_gather(grad_rows, "ch", axis=0, tiled=True),
    )
    hidden, preact_grad = pointwise_back(mixed_all, grad_all, w_in, w_out)
    w_in_local = contract_last(mixed_all, preact_grad)
    w_out_local = contract_last(grad_all, hidden)
    mix_grad = lax.psum_scatter(
        jnp.dot(w_in, preact_grad, preferred_element_type=jnp.float32),
        "ch",
        scatter_dimension=0,
        tiled=True,
    ).astype(jnp.bfloat16)
    w_in_sum, w_out_sum = (
        lax.psum_scatter(w_in_local, "sp", scatter_dimension=1, tiled=True),
        lax.psum_scatter(w_out_local, "sp", scatter_dimension=1, tiled=True),
    )
    mix_grad = mix_grad.reshape(local_ch, rows, width)
    rimmed = with_halo(mix_grad, (("sp", 1),), half)
    padded = jnp.pad(rimmed, ((0, 0), (0, 0), (half, half)))
    in_grad = out_grad.astype(jnp.float32) + depthwise(padded, kernel[:, ::-1, ::-1])
    kernel_part = depthwise(padded, features)
    kernel_grad = lax.psum(kernel_part, "sp")[:, ::-1, ::-1] * factor
    return (in_grad, kernel_grad, w_in_sum * factor, w_out_sum.T * factor)


def solution(mesh):
    return jax.shard_map(
        per_device,
        mesh=mesh,
        in_specs=(
            P(("grp", "ch"), "sp", None),
            P(("grp", "ch"), "sp", None),
            P(("grp", "ch"), "sp", None),
            P("ch", None, None),
            P(None, "ch"),
            P("ch", None),
        ),
        out_specs=(
            P(("grp", "ch"), "sp", None),
            P(("grp", "ch"), None, None),
            P("grp", ("ch", "sp")),
            P(("grp", "ch", "sp"), None),
        ),
        check_vma=False,
    )
```

profile of v0, /device:TPU:0, one launch (start us, length us, event | category | flops | bytes accessed | tf_op | source)
XLA Modules:
  0.0 533.9 jit_solution(92826388484412066)
XLA Ops:
  7.2 2.0 copy.34
  9.3 2.0 copy.35
  11.4 24.1 %all-gather.5.cloned.1.call-done = bf16[512,2048]{1,0:T(8,128)(2,1)} async-done(((bf16[128,2048]{1,0:T(8,128)(2,1)}), bf16[512,2048]{1,0:T(8,128)(2,1)}) %all-gather.5.cloned.1.call-update) | async-done | bytes 2097168 | tf_op jit(solution)/shard_map/all_gather | solution.py:66
  35.5 4.8 fusion.21
  40.3 19.3 %all-gather.3.cloned.1.call-done = bf16[512,2048]{1,0:T(8,128)(2,1)} async-done(((bf16[128,2048]{1,0:T(8,128)(2,1)}), bf16[512,2048]{1,0:T(8,128)(2,1)}) %all-gather.3.cloned.1.call-update) | async-done | bytes 2097168 | tf_op jit(solution)/shard_map/all_gather | solution.py:67
  59.7 4.6 fusion.5
  64.3 3.3 convolution_bitcast_fusion
  67.6 3.9 convolution_bitcast_fusion.1
  71.6 5.8 %fusion.18 = f32[512,512]{0,1:T(8,128)} fusion(bf16[512,2048]{1,0:T(8,128)(2,1)} %all-gather.3.cloned.1.call-done, f32[512,2048]{1,0:T(8,128)} %fusion.21), kind=kOutput, calls=%fused_computation.24 | convolution fusion | flops 1078984704 | bytes 7340032 | tf_op jit(solution)/shard_map/dot_general | solution.py:37
  77.5 34.7 %reduce-scatter.4.cloned.1.call-done = f32[128,2048]{0,1:T(8,128)} async-done(((f32[512,2048]{0,1:T(8,128)}), f32[128,2048]{0,1:T(8,128)}) %reduce-scatter.4.cloned.1.call-update) | async-done | bytes 1048592 | tf_op jit(solution)/shard_map/reduce_scatter | solution.py:72
  112.2 1.3 convert_element_type.16
  113.5 1.0 fusion.20
  114.5 3.4 collective-permute-start
  117.9 1.5 collective-permute-start.1
  119.4 1.2 copy.15
  121.5 1.5 copy.19
  123.0 28.5 %reduce-scatter.6.cloned.1.call-done = f32[512,128]{0,1:T(8,128)} async-done(((f32[512,512]{0,1:T(8,128)}), f32[512,128]{0,1:T(8,128)}) %reduce-scatter.6.cloned.1.call-update) | async-done | bytes 262160 | tf_op jit(solution)/shard_map/reduce_scatter | solution.py:79
  153.3 25.4 %reduce-scatter.8.cloned.1.call-done = f32[512,128]{0,1:T(8,128)} async-done(((f32[512,512]{0,1:T(8,128)}), f32[512,128]{0,1:T(8,128)}) %reduce-scatter.8.cloned.1.call-update) | async-done | bytes 262160 | tf_op jit(solution)/shard_map/reduce_scatter | solution.py:80
  178.7 1.8 multiply_bitcast_fusion
  181.2 1.8 fusion.17
  183.0 173.5 %fusion.7 = f32[1,128,31,31]{1,0,3,2:T(1,128)S(1)} fusion(bf16[128,1,16,128]{0,1,3,2:T(2,128)(2,1)S(1)} %copy-done.3, bf16[1,128,46,158]{1,3,2,0:T(8,128)(2,1)S(1)} %fusion.17), kind=kOutput, calls=%fused_computation.13 | convolution fusion | flops 503840768 | bytes 2876928 | tf_op jit(solution)/shard_map/conv_general_dilated | solution.py:25
  357.6 166.1 %fusion.9 = f32[1,128,16,128]{1,0,3,2:T(1,128)S(1)} fusion(bf16[1,128,46,158]{1,3,2,0:T(8,128)(2,1)S(1)} %fusion.17, bf16[128,1,31,31]{0,3,2,1:T(8,128)(2,1)} %bitcast.44), kind=kOutput, calls=%fused_computation.15 | convolution fusion | flops 503840768 | bytes 3155200 | tf_op jit(solution)/shard_map/conv_general_dilated | solution.py:25
  523.8 1.4 copy.20
  525.2 1.9 broadcast_multiply_fusion
  (37 shorter events, 4.9 us)
Async XLA Ops:
  7.2 28.3 %copy-start = (bf16[512,512]{1,0:T(8,128)(2,1)S(1)}, bf16[512,512]{1,0:T(8,128)(2,1)}, u32[]{:S(2)}) copy-start(bf16[512,512]{1,0:T(8,128)(2,1)} %param.10) | copy-start | bytes 1572868
  7.2 28.3 %all-gather.5.cloned.1.call-start = ((), (), s32[]{:S(2)}) async-start(), calls=%async_computation.4 | async-start | bytes 2621440 | tf_op jit(solution)/shard_map/all_gather | solution.py:66
  9.3 50.4 %all-gather.3.cloned.1.call-start = ((), (), s32[]{:S(2)}) async-start(), calls=%async_computation.3 | async-start | bytes 2621440 | tf_op jit(solution)/shard_map/all_gather | solution.py:67
  11.3 48.4 %copy-start.7 = (bf16[512,512]{1,0:T(8,128)(2,1)S(1)}, bf16[512,512]{1,0:T(8,128)(2,1)}, u32[]{:S(2)}) copy-start(bf16[512,512]{1,0:T(8,128)(2,1)} %param.11) | copy-start | bytes 1572868
  11.3 100.9 %reduce-scatter.4.cloned.1.call-start = ((), (), s32[]{:S(2)}) async-start(), calls=%async_computation.5 | async-start | bytes 5242880 | tf_op jit(solution)/shard_map/reduce_scatter | solution.py:72
  67.6 83.9 %reduce-scatter.6.cloned.1.call-start = ((), (), s32[]{:S(2)}) async-start(), calls=%async_computation.7 | async-start | bytes 1310720 | tf_op jit(solution)/shard_map/reduce_scatter | solution.py:79
  71.6 107.1 %reduce-scatter.8.cloned.1.call-start = ((), (), s32[]{:S(2)}) async-start(), calls=%async_computation.8 | async-start | bytes 1310720 | tf_op jit(solution)/shard_map/reduce_scatter | solution.py:80
  77.4 42.0 %copy-start.2 = (bf16[128,16,128]{2,1,0:T(8,128)(2,1)S(1)}, bf16[128,16,128]{2,1,0:T(8,128)(2,1)}, u32[]{:S(2)}) copy-start(bf16[128,16,128]{2,1,0:T(8,128)(2,1)} %param.8) | copy-start | bytes 1572868
  77.4 43.2 %copy-start.6 = (bf16[128,31,31]{0,2,1:T(8,128)(2,1)S(1)}, bf16[128,31,31]{0,2,1:T(8,128)(2,1)}, u32[]{:S(2)}) copy-start(bf16[128,31,31]{0,2,1:T(8,128)(2,1)} %param.9) | copy-start | bytes 738052
  77.4 44.1 %copy-start.4 = (bf16[128,16,128]{2,1,0:T(8,128)(2,1)S(1)}, bf16[128,16,128]{2,1,0:T(8,128)(2,1)}, u32[]{:S(2)}) copy-start(bf16[128,16,128]{2,1,0:T(8,128)(2,1)} %param.6) | copy-start | bytes 1572868
  77.5 447.7 %all-reduce.3.cloned.1.call-start = ((), (), s32[]{:S(2)}) async-start(), calls=%async_computation.6 | async-start | bytes 1015808 | tf_op jit(solution)/shard_map/psum | solution.py:87
  114.5 65.9 %collective-permute-start = (bf16[128,15,128]{0,2,1:T(8,128)(2,1)}, bf16[128,15,128]{0,2,1:T(8,128)(2,1)S(1)}, u32[]{:S(2)}, u32[]{:S(2)}) collective-permute-start(bf16[128,15,128]{0,2,1:T(8,128)(2,1)} %get-tuple-element.12), channel_id=1, source_target_pairs={{0,1},{1,2},{2,3},{4,5},{5,6},{6,7},{8,9},{9,10},{10,11},{12,13},{... | collective-permute-start | bytes 1474568 | tf_op jit(solution)/shard_map/ppermute | solution.py:16
  117.9 63.3 %collective-permute-start.1 = (bf16[128,15,128]{0,2,1:T(8,128)(2,1)S(1)}, bf16[128,15,128]{0,2,1:T(8,128)(2,1)}, u32[]{:S(2)}, u32[]{:S(2)}) collective-permute-start(bf16[128,15,128]{0,2,1:T(8,128)(2,1)S(1)} %get-tuple-element.13), channel_id=1, source_target_pairs={{1,0},{2,1},{3,2},{5,4},{6,5},{7,6},{9,8},{10,9},{11,10},{13,12},{... | collective-permute-start | bytes 1474568 | tf_op jit(solution)/shard_map/ppermute | solution.py:19
  178.7 4.3 copy-start.3
  180.4 0.8 copy-start.5
  357.5 166.1 %copy-start.1 = (bf16[128,16,128]{0,2,1:T(8,128)(2,1)S(1)}, bf16[128,16,128]{0,2,1:T(8,128)(2,1)}, u32[]{:S(2)}) copy-start(bf16[128,16,128]{0,2,1:T(8,128)(2,1)} %copy.15) | copy-start | bytes 1572868
Sparse Core Ops, SparseCore 0:
  10.1 25.2 all-gather.4
  37.0 22.5 all-gather.2
  67.7 44.4 reduce-scatter.3
  114.5 36.9 reduce-scatter.5
  153.6 25.0 reduce-scatter.7
  357.7 36.7 all-reduce.2
where the time goes:
time: 534 us
  matrix products  362 us (68%)
  waiting for transfers between devices  132 us (25%)
  between operations  14.2 us (3%)
  local copies, waits for them, and re-layouts  12.6 us (2%)
  other arithmetic  7.77 us (1%)
    conv_general_dilated x2, matrix products, depthwise(): lax.conv_general_dilated(source[None], taps[:, None], (1, 1), 'VALID', di...  340 us
    reduce_scatter x1, waiting for transfers between devices, per_device(): lax.psum_scatter(jnp.dot(w_in, preact_grad, preferred_element_type=jnp.fl...  34.7 us
    reduce_scatter x1, waiting for transfers between devices, per_device(): lax.psum_scatter(w_in_local, 'sp', scatter_dimension=1, tiled=True)  28.5 us
    reduce_scatter x1, waiting for transfers between devices, per_device(): lax.psum_scatter(w_out_local, 'sp', scatter_dimension=1, tiled=True)  25.4 us
    all_gather x1, waiting for transfers between devices, per_device(): lax.all_gather(mixed_rows, 'ch', axis=0, tiled=True)  24.1 us
    all_gather x1, waiting for transfers between devices, per_device(): lax.all_gather(grad_rows, 'ch', axis=0, tiled=True)  19.3 us
  transfers between devices with their start and end apart: 8, of which 5 were waited for; matrix products, arithmetic and copies ran while one was open for 36% of the time, Pallas kernels for 0%

commit v1 on v0

--- a/solution.py
+++ b/solution.py
@@ -6,6 +6,22 @@
 
 SQRT_HALF = 0.7071067811865476
 INV_ROOT_TAU = 0.3989422804014327
+
+
+def gather_around(x, axis, dim):
+    ways, here, hop = (lax.axis_size(axis), lax.axis_index(axis), x.shape[dim])
+    lengths = [n * ways if d == dim else n for d, n in enumerate(x.shape)]
+    full = lax.dynamic_update_slice_in_dim(jnp.zeros(lengths, x.dtype), x, here * hop, axis=dim)
+    going_up = going_down = x
+    for far in range(1, ways // 2 + 1):
+        going_up = lax.ppermute(going_up, axis, [(d, (d + 1) % ways) for d in range(ways)])
+        full = lax.dynamic_update_slice_in_dim(full, going_up, (here - far) % ways * hop, axis=dim)
+        if 2 * far < ways:
+            going_down = lax.ppermute(going_down, axis, [(d, (d - 1) % ways) for d in range(ways)])
+            full = lax.dynamic_update_slice_in_dim(
+                full, going_down, (here + far) % ways * hop, axis=dim
+            )
+    return full
 
 
 def with_halo(block, sides, width):
@@ -63,7 +79,7 @@
     mixed_rows = saved_mix.reshape(local_ch, local_pos)
     grad_rows = out_grad.reshape(local_ch, local_pos)
     mixed_all, grad_all = (
-        lax.all_gather(mixed_rows, "ch", axis=0, tiled=True),
+        gather_around(mixed_rows, "ch", 0),
         lax.all_gather(grad_rows, "ch", axis=0, tiled=True),
     )
     hidden, preact_grad = pointwise_back(mixed_all, grad_all, w_in, w_out)

time: 534 us -> 656 us (1.23)
  matrix products: 362 us -> 492 us
  waiting for transfers between devices: 132 us -> 111 us
  starting transfers between devices: 5.13 us -> 14.7 us
    conv_general_dilated x2, matrix products: 340 us -> 471 us  [depthwise(): lax.conv_general_dilated(source[None], taps[:, None], (1, 1), 'VALID', di...]
    all_gather x1 -> x0, waiting for transfers between devices: 24.1 us -> none  [per_device(): lax.all_gather(mixed_rows, 'ch', axis=0, tiled=True)]
    ppermute x0 -> x3, waiting for transfers between devices: none -> 19.8 us  [the longest x2 19.8 us: gather_around(): lax.ppermute(going_up, axis, [(d, (d + 1) % ways) for d in range(ways)])]
    all_gather x1, waiting for transfers between devices: 19.3 us -> 0.01 us  [per_device(): lax.all_gather(grad_rows, 'ch', axis=0, tiled=True)]
    ppermute x0 -> x3, starting transfers between devices: none -> 9.62 us  [the longest x2 7.67 us: gather_around(): lax.ppermute(going_up, axis, [(d, (d + 1) % ways) for d in range(ways)])]
  transfers between devices with their start and end apart: 8 -> 10, of which waited for: 5 -> 5; matrix products, arithmetic and copies ran while one was open for 36% -> 29% of each run, Pallas kernels for 0% -> 0%
where the time goes in v1:
time: 656 us
  matrix products  492 us (75%)
  waiting for transfers between devices  111 us (17%)
  local copies, waits for them, and re-layouts  16.8 us (3%)
  starting transfers between devices  14.7 us (2%)
  between operations  14 us (2%)
  other arithmetic  7.57 us (1%)
    conv_general_dilated x2, matrix products, depthwise(): lax.conv_general_dilated(source[None], taps[:, None], (1, 1), 'VALID', di...  471 us
    reduce_scatter x1, waiting for transfers between devices, per_device(): lax.psum_scatter(jnp.dot(w_in, preact_grad, preferred_element_type=jnp.fl...  37.4 us
    reduce_scatter x1, waiting for transfers between devices, per_device(): lax.psum_scatter(w_out_local, 'sp', scatter_dimension=1, tiled=True)  28.4 us
    reduce_scatter x1, waiting for transfers between devices, per_device(): lax.psum_scatter(w_in_local, 'sp', scatter_dimension=1, tiled=True)  25.4 us
    ppermute x2, waiting for transfers between devices, gather_around(): lax.ppermute(going_up, axis, [(d, (d + 1) % ways) for d in range(ways)])  19.8 us
  transfers between devices with their start and end apart: 10, of which 5 were waited for; matrix products, arithmetic and copies ran while one was open for 29% of the time, Pallas kernels for 0%

profile of v1, /device:TPU:0, one launch (start us, length us, event | category | flops | bytes accessed | tf_op | source)
XLA Modules:
  0.0 655.9 jit_solution(4315637692534376841)
XLA Ops:
  7.2 2.0 copy.43
  9.3 2.0 copy.42
  11.8 2.0 collective-permute-start.1
  13.8 11.7 %collective-permute-done = bf16[128,2048]{1,0:T(8,128)(2,1)} collective-permute-done((bf16[128,2048]{1,0:T(8,128)(2,1)}, bf16[128,2048]{1,0:T(8,128)(2,1)}, u32[]{:S(2)}, u32[]{:S(2)}) %collective-permute-start) | collective-permute-done | bytes 524320 | tf_op jit(solution)/shard_map/ppermute | solution.py:17
  25.4 7.2 %collective-permute-start.2 = (bf16[128,2048]{1,0:T(8,128)(2,1)}, bf16[128,2048]{1,0:T(8,128)(2,1)}, u32[]{:S(2)}, u32[]{:S(2)}) collective-permute-start(bf16[128,2048]{1,0:T(8,128)(2,1)} %collective-permute-done), channel_id=1, source_target_pairs={{0,4},{4,8},{8,12},{12,0},{1,5},{5,9},{9,13},{13,1},{2,6},{6,10},{... | collective-permute-start | bytes 1572872 | tf_op jit(solution)/shard_map/ppermute | solution.py:17
  35.3 8.1 %collective-permute-done.2 = bf16[128,2048]{1,0:T(8,128)(2,1)} collective-permute-done((bf16[128,2048]{1,0:T(8,128)(2,1)}, bf16[128,2048]{1,0:T(8,128)(2,1)}, u32[]{:S(2)}, u32[]{:S(2)}) %collective-permute-start.2) | collective-permute-done | bytes 524320 | tf_op jit(solution)/shard_map/ppermute | solution.py:17
  44.5 3.3 fusion.29
  47.8 4.6 fusion.5
  52.4 1.3 copy-done.1
  53.7 3.3 convolution_bitcast_fusion
  57.1 5.2 fusion.23
  62.4 3.9 fusion.30
  66.3 37.4 %reduce-scatter.4.cloned.1.call-done = f32[128,2048]{0,1:T(8,128)} async-done(((f32[512,2048]{0,1:T(8,128)}), f32[128,2048]{0,1:T(8,128)}) %reduce-scatter.4.cloned.1.call-update) | async-done | bytes 1048592 | tf_op jit(solution)/shard_map/reduce_scatter | solution.py:88
  106.1 3.4 collective-permute-start.3
  109.5 1.5 collective-permute-start.4
  113.1 1.5 copy.22
  114.6 28.4 %reduce-scatter.8.cloned.1.call-done = f32[512,128]{1,0:T(8,128)} async-done(((f32[512,512]{1,0:T(8,128)}), f32[512,128]{1,0:T(8,128)}) %reduce-scatter.8.cloned.1.call-update) | async-done | bytes 262160 | tf_op jit(solution)/shard_map/reduce_scatter | solution.py:96
  144.8 25.4 %reduce-scatter.6.cloned.1.call-done = f32[512,128]{1,0:T(8,128)} async-done(((f32[512,512]{1,0:T(8,128)}), f32[512,128]{1,0:T(8,128)}) %reduce-scatter.6.cloned.1.call-update) | async-done | bytes 262160 | tf_op jit(solution)/shard_map/reduce_scatter | solution.py:95
  170.2 1.7 broadcast_multiply_fusion.1
  171.9 1.7 fusion.22
  173.6 307.1 %fusion.11 = f32[1,128,31,31]{1,0,3,2:T(1,128)S(1)} fusion(bf16[128,1,16,128]{0,1,3,2:T(2,128)(2,1)} %copy.22, bf16[1,128,46,158]{1,3,2,0:T(8,128)(2,1)S(1)} %fusion.22), kind=kOutput, calls=%fused_computation.17 | convolution fusion | flops 503840768 | bytes 2876928 | tf_op jit(solution)/shard_map/conv_general_dilated | solution.py:41
  481.7 164.2 %fusion.13 = f32[1,128,16,128]{1,0,3,2:T(1,128)S(1)} fusion(bf16[1,128,46,158]{1,3,2,0:T(8,128)(2,1)S(1)} %fusion.22, bf16[128,1,31,31]{0,3,2,1:T(8,128)(2,1)S(1)} %bitcast.64), kind=kOutput, calls=%fused_computation.19 | convolution fusion | flops 503840768 | bytes 3155200 | tf_op jit(solution)/shard_map/conv_general_dilated | solution.py:41
  646.1 1.4 copy.24
  647.5 1.9 broadcast_multiply_fusion
  (47 shorter events, 11.7 us)
Async XLA Ops:
  7.2 37.3 %copy-start = (bf16[512,512]{1,0:T(8,128)(2,1)S(1)}, bf16[512,512]{1,0:T(8,128)(2,1)}, u32[]{:S(2)}) copy-start(bf16[512,512]{1,0:T(8,128)(2,1)} %param.10) | copy-start | bytes 1572868
  7.2 40.6 %all-gather.2.cloned.1.call-start = ((), (), s32[]{:S(2)}) async-start(), calls=%async_computation.3 | async-start | bytes 2621440 | tf_op jit(solution)/shard_map/all_gather | solution.py:83
  9.3 23.6 %copy-start.3 = (bf16[128,16,128]{2,1,0:T(8,128)(2,1)S(1)}, bf16[128,16,128]{2,1,0:T(8,128)(2,1)}, u32[]{:S(2)}) copy-start(bf16[128,16,128]{2,1,0:T(8,128)(2,1)} %param.7) | copy-start | bytes 1572868
  9.3 94.5 %reduce-scatter.4.cloned.1.call-start = ((), (), s32[]{:S(2)}) async-start(), calls=%async_computation.4 | async-start | bytes 5242880 | tf_op jit(solution)/shard_map/reduce_scatter | solution.py:88
  11.4 14.1 %collective-permute-start = (bf16[128,2048]{1,0:T(8,128)(2,1)}, bf16[128,2048]{1,0:T(8,128)(2,1)}, u32[]{:S(2)}, u32[]{:S(2)}) collective-permute-start(bf16[128,2048]{1,0:T(8,128)(2,1)} %bitcast.52), channel_id=1, source_target_pairs={{0,4},{4,8},{8,12},{12,0},{1,5},{5,9},{9,13},{13,1},{2,6},{6,10},{... | collective-permute-start | bytes 1572872 | tf_op jit(solution)/shard_map/ppermute | solution.py:17
  11.8 22.4 %collective-permute-start.1 = (bf16[128,2048]{1,0:T(8,128)(2,1)}, bf16[128,2048]{1,0:T(8,128)(2,1)}, u32[]{:S(2)}, u32[]{:S(2)}) collective-permute-start(bf16[128,2048]{1,0:T(8,128)(2,1)} %bitcast.52), channel_id=1, source_target_pairs={{0,12},{4,0},{8,4},{12,8},{1,13},{5,1},{9,5},{13,9},{2,14},{6,2},{... | collective-permute-start | bytes 1572872 | tf_op jit(solution)/shard_map/ppermute | solution.py:20
  25.4 18.0 %collective-permute-start.2 = (bf16[128,2048]{1,0:T(8,128)(2,1)}, bf16[128,2048]{1,0:T(8,128)(2,1)}, u32[]{:S(2)}, u32[]{:S(2)}) collective-permute-start(bf16[128,2048]{1,0:T(8,128)(2,1)} %collective-permute-done), channel_id=1, source_target_pairs={{0,4},{4,8},{8,12},{12,0},{1,5},{5,9},{9,13},{13,1},{2,6},{6,10},{... | collective-permute-start | bytes 1572872 | tf_op jit(solution)/shard_map/ppermute | solution.py:17
  44.5 3.3 copy-start.8
  52.4 1.3 copy-start.1
  57.1 85.9 %reduce-scatter.8.cloned.1.call-start = ((), (), s32[]{:S(2)}) async-start(), calls=%async_computation.7 | async-start | bytes 1310720 | tf_op jit(solution)/shard_map/reduce_scatter | solution.py:96
  62.4 107.9 %reduce-scatter.6.cloned.1.call-start = ((), (), s32[]{:S(2)}) async-start(), calls=%async_computation.6 | async-start | bytes 1310720 | tf_op jit(solution)/shard_map/reduce_scatter | solution.py:95
  66.3 44.7 %copy-start.4 = (bf16[128,16,128]{2,1,0:T(8,128)(2,1)S(1)}, bf16[128,16,128]{2,1,0:T(8,128)(2,1)}, u32[]{:S(2)}) copy-start(bf16[128,16,128]{2,1,0:T(8,128)(2,1)} %param.8) | copy-start | bytes 1572868
  66.3 45.9 %copy-start.6 = (bf16[128,31,31]{0,2,1:T(8,128)(2,1)S(1)}, bf16[128,31,31]{0,2,1:T(8,128)(2,1)}, u32[]{:S(2)}) copy-start(bf16[128,31,31]{0,2,1:T(8,128)(2,1)} %param.9) | copy-start | bytes 738052
  66.3 581.2 %all-reduce.3.cloned.1.call-start = ((), (), s32[]{:S(2)}) async-start(), calls=%async_computation.5 | async-start | bytes 1015808 | tf_op jit(solution)/shard_map/psum | solution.py:103
  105.0 8.1 %copy-start.5 = (bf16[128,16,128]{2,1,0:T(8,128)(2,1)S(1)}, bf16[128,16,128]{2,1,0:T(8,128)(2,1)}, u32[]{:S(2)}) copy-start(bf16[128,16,128]{2,1,0:T(8,128)(2,1)} %param.6) | copy-start | bytes 1572868
  106.1 65.8 %collective-permute-start.3 = (bf16[128,15,128]{0,2,1:T(8,128)(2,1)}, bf16[128,15,128]{0,2,1:T(8,128)(2,1)S(1)}, u32[]{:S(2)}, u32[]{:S(2)}) collective-permute-start(bf16[128,15,128]{0,2,1:T(8,128)(2,1)} %get-tuple-element.12), channel_id=1, source_target_pairs={{0,1},{1,2},{2,3},{4,5},{5,6},{6,7},{8,9},{9,10},{10,11},{12,13},{... | collective-permute-start | bytes 1474568 | tf_op jit(solution)/shard_map/ppermute | solution.py:32
  109.5 62.4 %collective-permute-start.4 = (bf16[128,15,128]{0,2,1:T(8,128)(2,1)S(1)}, bf16[128,15,128]{0,2,1:T(8,128)(2,1)}, u32[]{:S(2)}, u32[]{:S(2)}) collective-permute-start(bf16[128,15,128]{0,2,1:T(8,128)(2,1)S(1)} %get-tuple-element.13), channel_id=1, source_target_pairs={{1,0},{2,1},{3,2},{5,4},{6,5},{7,6},{9,8},{10,9},{11,10},{13,12},{... | collective-permute-start | bytes 1474568 | tf_op jit(solution)/shard_map/ppermute | solution.py:35
  480.7 1.0 copy-start.7
  481.7 164.2 %copy-start.2 = (bf16[128,16,128]{0,2,1:T(8,128)(2,1)S(1)}, bf16[128,16,128]{0,2,1:T(8,128)(2,1)}, u32[]{:S(2)}) copy-start(bf16[128,16,128]{0,2,1:T(8,128)(2,1)} %copy.17) | copy-start | bytes 1572868
Sparse Core Ops, SparseCore 0:
  9.6 33.3 all-gather.1
  57.2 46.5 reduce-scatter.3
  106.2 36.7 reduce-scatter.7
  145.1 25.0 reduce-scatter.5
  481.8 36.7 all-reduce.2
